TPU v7x, 256 devices: a whole 4x4x8 slice. The times are simulated.
256 devices in a mesh: tiles: 64 (over x, y_lo, z), fblk: 4 (over y_hi, core).
Axes of the slice: x: 4, y: 4 (y_hi: 2, y_lo: 2; y = y_hi * 2 + y_lo), z: 8, core: 2. Of those that a mesh axis runs over, the one named last changes fastest.
Arguments:
- images: float32 [64, 48, 128], P('tiles'), may hold values from -6 to 6
- sparse_codes: bfloat16 [64, 256, 48, 128], P('tiles', 'fblk'), may hold values from -0.5 to 0.5
- filters: float32 [256, 11, 11], P('fblk'), may hold values from -0.5 to 0.5
- plan: int32 [4], replicated, may hold values from 0 to 3, as said below
Outputs:
- filters_out: float32 [256, 11, 11], P('fblk')
- codes_out: bfloat16 [64, 256, 48, 128], P('tiles', 'fblk')
Inputs may be any that keep to these rules, and one draw needn't show every extreme that they name: `plan`: names every filter block exactly once, in some order.
All inputs are finite; a program needn't handle non-finite values.
Results may differ from a plain program's by a relative error of at most 0.01.
Values sent between devices are 32-bit elements; how exact they have to be, the bound alone decides.
A program may use at most 64 MiB of HBM per device.

v0:
```python
import jax
import jax.numpy as jnp
from jax import lax
from jax.sharding import PartitionSpec as P

STEPS = 4


step_filter = 128.0
step_code = 0.05
shrink_level = 0.02


def spread(tap_maps, height, breadth):
    padded = jnp.pad(tap_maps, ((0, 0), (0, 0), (5, 5), (5, 5)))
    summed = jnp.zeros((tap_maps.shape[0], height, breadth), jnp.float32)
    for row_tap in range(11):
        for col_tap in range(11):
            summed = (
                summed
                + padded[
                    :,
                    row_tap * 11 + col_tap,
                    row_tap : row_tap + height,
                    col_tap : col_tap + breadth,
                ]
            )
    return summed


def shifted(resid):
    height, breadth = (resid.shape[1], resid.shape[2])
    padded = jnp.pad(resid, ((0, 0), (5, 5), (5, 5)))
    pieces = []
    for row_tap in range(11):
        for col_tap in range(11):
            pieces.append(
                padded[
                    :, 10 - row_tap : 10 - row_tap + height, 10 - col_tap : 10 - col_tap + breadth
                ]
            )
    return jnp.stack(pieces, axis=1).astype(jnp.bfloat16)


def synthesize(weights_bf, flat_codes, height, breadth):
    tap_maps = jnp.einsum("ko,tkp->top", weights_bf, flat_codes, preferred_element_type=jnp.float32)
    return spread(tap_maps.reshape(flat_codes.shape[0], 121, height, breadth), height, breadth)


def renorm(values):
    return values / jnp.sqrt(jnp.sum(values * values, axis=1, keepdims=True) + 1e-06)


def body(images, sparse_codes, filters, plan):
    tile_count, channels, height, breadth = sparse_codes.shape
    pixels = float(lax.axis_size("tiles") * tile_count * height * breadth)
    flat_filters = filters.reshape(channels, 121)
    codes_now = sparse_codes
    for step_index in range(STEPS):
        block_id = plan[step_index]
        is_owner = lax.axis_index("fblk") == block_id
        flat_codes = codes_now.reshape(tile_count, channels, height * breadth)
        partial_old = synthesize(flat_filters.astype(jnp.bfloat16), flat_codes, height, breadth)
        residual = lax.psum(partial_old, "fblk") - images
        shift_maps = shifted(residual).reshape(tile_count, 121, height * breadth)
        grad_part = jnp.einsum(
            "tkp,top->ko", flat_codes, shift_maps, preferred_element_type=jnp.float32
        )
        grad_sum = lax.psum(grad_part, "tiles")
        renewed = renorm(flat_filters - step_filter * grad_sum / pixels)
        flat_filters = jnp.where(is_owner, renewed, flat_filters)
        new_bf = flat_filters.astype(jnp.bfloat16)
        partial_new = synthesize(new_bf, flat_codes, height, breadth)
        residual_new = lax.psum(partial_new, "fblk") - images
        shift_new = shifted(residual_new).reshape(tile_count, 121, height * breadth)
        grad_code = jnp.einsum("ko,top->tkp", new_bf, shift_new, preferred_element_type=jnp.float32)
        moved = codes_now.astype(jnp.float32) - step_code * grad_code.reshape(codes_now.shape)
        codes_now = (moved - jnp.clip(moved, -shrink_level, shrink_level)).astype(jnp.bfloat16)
    return (flat_filters.reshape(channels, 11, 11), codes_now)


def solution(mesh):
    in_specs = (P("tiles", None, None), P("tiles", "fblk", None, None), P("fblk", None, None), P())
    out_specs = (P("fblk", None, None), P("tiles", "fblk", None, None))
    return jax.shard_map(body, mesh=mesh, in_specs=in_specs, out_specs=out_specs, check_vma=False)
```

profile of v0, /device:TPU:1, one launch (start us, length us, event | category | flops | bytes accessed | tf_op | source)
XLA Modules:
  0.0 1902.2 jit_solution(10064681667100212784)
XLA Ops:
  10.7 2.7 fusion.376
  13.4 15.7 psum.84
  56.0 14.3 stack.3049
  71.0 255.3 %psum.85 = f32[64,121]{1,0:T(8,128)S(1)} all-reduce(f32[64,121]{1,0:T(8,128)S(1)} %convolution_bitcast_fusion), channel_id=1, replica_groups=mesh['tiles'=64,'fblk'=4] {'tiles'}, use_global_device_ids=true, to_apply=%region_1.2 | all-reduce | flops 7744 | bytes 61952 | tf_op jit(solution)/shard_map/psum | solution.py:69
  328.8 70.2 %psum.86 = f32[1,48,128]{2,1,0:T(8,128)S(1)} all-reduce(f32[1,48,128]{2,1,0:T(8,128)S(1)} %fusion.583), channel_id=1, replica_groups=mesh['tiles'=64,'fblk'=4] {'fblk'}, use_global_device_ids=true, to_apply=%region_3.4 | all-reduce | flops 6144 | bytes 49152 | tf_op jit(solution)/shard_map/psum | solution.py:74
  447.7 14.3 stack.3171
  465.2 3.6 copy.27
  468.8 2.7 fusion.790
  471.5 21.7 %psum.87 = f32[1,48,128]{2,1,0:T(8,128)S(1)} all-reduce(f32[1,48,128]{2,1,0:T(8,128)S(1)} %fusion.790), channel_id=1, replica_groups=mesh['tiles'=64,'fblk'=4] {'fblk'}, use_global_device_ids=true, to_apply=%region_4.5 | all-reduce | flops 6144 | bytes 49152 | tf_op jit(solution)/shard_map/psum | solution.py:64
  541.9 14.3 stack.3293
  556.9 247.8 %psum.88 = f32[64,121]{1,0:T(8,128)S(1)} all-reduce(f32[64,121]{1,0:T(8,128)S(1)} %fusion.22), channel_id=1, replica_groups=mesh['tiles'=64,'fblk'=4] {'tiles'}, use_global_device_ids=true, to_apply=%region_5.6 | all-reduce | flops 7744 | bytes 61952 | tf_op jit(solution)/shard_map/psum | solution.py:69
  807.2 3.6 copy.29
  810.8 2.7 fusion.997
  813.5 69.8 %psum.89 = f32[1,48,128]{2,1,0:T(8,128)S(1)} all-reduce(f32[1,48,128]{2,1,0:T(8,128)S(1)} %fusion.997), channel_id=1, replica_groups=mesh['tiles'=64,'fblk'=4] {'fblk'}, use_global_device_ids=true, to_apply=%region_7.8 | all-reduce | flops 6144 | bytes 49152 | tf_op jit(solution)/shard_map/psum | solution.py:74
  932.0 14.3 stack.3415
  949.5 3.6 copy.31
  953.2 2.7 fusion.1204
  955.8 13.7 psum.90
  1018.2 14.3 stack.3537
  1033.2 248.0 %psum.91 = f32[64,121]{1,0:T(8,128)S(1)} all-reduce(f32[64,121]{1,0:T(8,128)S(1)} %fusion.16), channel_id=1, replica_groups=mesh['tiles'=64,'fblk'=4] {'tiles'}, use_global_device_ids=true, to_apply=%region_9.10 | all-reduce | flops 7744 | bytes 61952 | tf_op jit(solution)/shard_map/psum | solution.py:69
  1283.7 3.6 copy.33
  1287.4 2.7 fusion.1411
  1290.0 69.8 %psum.92 = f32[1,48,128]{2,1,0:T(8,128)S(1)} all-reduce(f32[1,48,128]{2,1,0:T(8,128)S(1)} %fusion.1411), channel_id=1, replica_groups=mesh['tiles'=64,'fblk'=4] {'fblk'}, use_global_device_ids=true, to_apply=%region_11.12 | all-reduce | flops 6144 | bytes 49152 | tf_op jit(solution)/shard_map/psum | solution.py:74
  1408.5 14.3 stack.3659
  1426.0 3.6 copy.35
  1429.7 2.7 fusion.1618
  1432.4 13.5 psum.93
  1494.5 14.3 stack.3781
  1509.5 247.9 %psum.94 = f32[64,121]{1,0:T(8,128)S(1)} all-reduce(f32[64,121]{1,0:T(8,128)S(1)} %fusion.10), channel_id=1, replica_groups=mesh['tiles'=64,'fblk'=4] {'tiles'}, use_global_device_ids=true, to_apply=%region_13.14 | all-reduce | flops 7744 | bytes 61952 | tf_op jit(solution)/shard_map/psum | solution.py:69
  1760.7 3.6 copy.38
  1767.0 70.0 %psum.95 = f32[1,48,128]{2,1,0:T(8,128)S(1)} all-reduce(f32[1,48,128]{2,1,0:T(8,128)S(1)} %fusion.1825), channel_id=1, replica_groups=mesh['tiles'=64,'fblk'=4] {'fblk'}, use_global_device_ids=true, to_apply=%region_15.16 | all-reduce | flops 6144 | bytes 49152 | tf_op jit(solution)/shard_map/psum | solution.py:74
  1885.6 14.3 stack.3903
  (1034 shorter events, 399.1 us)
Async XLA Ops:
  10.7 18.4 copy-start.1
  37.4 18.5 copy-start.2
  56.0 14.3 copy-start
where the time goes:
time: 1920 us; the launch traced here: 1900 us
  blocking collectives  1340 us (70%)
  local copies, waits for them, and re-layouts  508 us (26%)
  other arithmetic  23 us (1%)
  matrix products  20.1 us (1%)
    psum x4, blocking collectives, body(): grad_sum = lax.psum(grad_part, 'tiles')  999 us
    unnamed x915, local copies, waits for them, and re-layouts  340 us
    psum x4, blocking collectives, body(): residual_new = lax.psum(partial_new, 'fblk') - images  280 us
    another operation x68, local copies, waits for them, and re-layouts, shifted(): return jnp.stack(pieces, axis=1).astype(jnp.bfloat16)  140 us
    psum x4, blocking collectives, body(): residual = lax.psum(partial_old, 'fblk') - images  64.6 us

commit v1 on v0

v1 whole, which is shorter than its diff:
```python
import jax
import jax.numpy as jnp
from jax import lax
from jax.experimental import pallas as pl
from jax.experimental.pallas import tpu as pltpu
from jax.sharding import PartitionSpec as P

STEPS = 4
TAPS = 11
H, W = 48, 128
PIX = H * W
KB = 64
HALF = KB // 2
COLS = 16 * TAPS
PAD = 5 * W
CODE_LANES = 60 * W
SHIFT_LANES = PIX + 2 * PAD
GROUPS = 3
MAP_LANES = 56 * W
CHUNK = 512
ROWS = CHUNK // W

step_filter = 128.0
step_code = 0.05
shrink_level = 0.02
MESH = pl.DeviceIdType.MESH
F32, BF16 = jnp.float32, jnp.bfloat16


def flip(index, mask):
    out = index
    bit = 1
    while bit <= mask:
        if mask & bit:
            out = out + bit * (1 - 2 * ((index // bit) % 2))
        bit *= 2
    return out


def tree_sum(parts):
    while len(parts) > 1:
        parts = [
            parts[i] + parts[i + 1] if i + 1 < len(parts) else parts[i]
            for i in range(0, len(parts), 2)
        ]
    return parts[0]


def nt_dot(a, b):
    return lax.dot_general(a, b, (((1,), (1,)), ((), ())), preferred_element_type=F32)


def kernel(
    plan, images, codes, filters, filters_out, codes_out,
    natural, held, maps, spread_mat, expand_mat, shifts, bank, parts, near, far, send, recv,
):
    tile, fblk = lax.axis_index("tiles"), lax.axis_index("fblk")
    z_peers = [(n, 0) for n in range(1, 8)]
    xy_peers = [(8 * n, 0) for n in range(1, 8)]
    group_peers = [(0, r) for r in range(1, 4)]
    peers = z_peers + xy_peers + group_peers

    def device(peer):
        return (flip(tile, peer[0]), flip(fblk, peer[1]))

    barrier = pltpu.get_barrier_semaphore()
    for peer in peers:
        pl.semaphore_signal(barrier, inc=1, device_id=device(peer), device_id_type=MESH)

    row = lax.broadcasted_iota(jnp.int32, (4 * GROUPS * 16, 128), 0)
    col = lax.broadcasted_iota(jnp.int32, (4 * GROUPS * 16, 128), 1)
    tap = (row + 5) & 15
    for r in range(4):
        first = r * GROUPS * 16
        line = ((row - first) >> 4) * 4 + r
        part = (tap < TAPS) & (line < TAPS) & (line * TAPS + 10 - tap == col)
        spread_mat[first : first + GROUPS * 16, :] = jnp.where(part, 1.0, 0.0).astype(BF16)[
            first : first + GROUPS * 16
        ]
    col = lax.broadcasted_iota(jnp.int32, (128, COLS), 0)
    row = lax.broadcasted_iota(jnp.int32, (128, COLS), 1)
    tap = (row + 5) & 15
    part = (tap < TAPS) & ((row >> 4) * TAPS + tap == col)
    expand_mat[...] = jnp.where(part, 1.0, 0.0).astype(BF16)
    held[:, 0:PAD] = jnp.zeros((KB, PAD), BF16)
    held[:, PAD + PIX : CODE_LANES] = jnp.zeros((KB, CODE_LANES - PAD - PIX), BF16)
    shifts[:, 0:PAD] = jnp.zeros((16, PAD), BF16)
    shifts[:, PAD + PIX : SHIFT_LANES] = jnp.zeros((16, PAD), BF16)
    bank[...] = filters[...]

    def unfold(k, carry):
        rows = pl.ds(pl.multiple_of(k * 8 * H, 8 * H), 8 * H)
        natural[rows, :] = codes[rows, :].astype(F32)
        return carry

    lax.fori_loop(0, KB // 8, unfold, 0)
    for y in range(H):
        held[:, PAD + y * W : PAD + (y + 1) * W] = natural[pl.ds(y, KB, stride=H), :].astype(BF16)

    tap = (lax.broadcasted_iota(jnp.int32, (16, W), 0) + 5) & 15
    lane = lax.broadcasted_iota(jnp.int32, (16, W), 1)
    source = lane - tap + 5
    inside = (tap < TAPS) & (source >= 0) & (source < W)

    def turn(front, back):
        front = pltpu.roll(front, 0, 1, stride=1, stride_axis=0)
        back = pltpu.roll(back, W - 8, 1, stride=1, stride_axis=0)
        return jnp.where(inside, jnp.concatenate([front, back], axis=0), 0.0)

    def synth(kind, s):
        @pl.when(tile >= 0)
        def _():
            slabs = nt_dot(spread_mat[...], bank[...].astype(BF16))
            weights = jnp.concatenate(
                [slabs[r * GROUPS * 16 : (r + 1) * GROUPS * 16] for r in range(4)], axis=1
            ).astype(BF16)
            lag = 3
            for c in range(H // ROWS + lag):
                at = c * CHUNK
                if at < MAP_LANES:
                    piled = jnp.concatenate(
                        [held[:, at + r * W : at + r * W + CHUNK] for r in range(4)], axis=0
                    )
                    maps[:, at : at + CHUNK] = jnp.dot(weights, piled, preferred_element_type=F32)
                if c >= lag:
                    for y in range((c - lag) * ROWS, (c - lag + 1) * ROWS):
                        total = tree_sum([
                            maps[g * 16 : (g + 1) * 16, (y + 4 * g) * W : (y + 4 * g + 1) * W]
                            for g in range(GROUPS)
                        ])
                        turned = turn(total[0:8], total[8:16])
                        parts[kind, s, 0, y : y + 1, :] = jnp.sum(turned, axis=0, keepdims=True)

    def copies(src, dst, q, s, n, peer):
        return pltpu.make_async_remote_copy(
            src_ref=src.at[s, 0], dst_ref=dst.at[s, n],
            send_sem=send.at[q, s], recv_sem=recv.at[q, s],
            device_id=device(peer), device_id_type=MESH,
        )

    def start(ref, q, s, targets):
        for n, peer in enumerate(targets):
            copies(ref, ref, q, s, n + 1, peer).start()

    def finish(ref, sem, q, s, count):
        got = ref.at[s, pl.ds(1, count)]
        pltpu.make_async_copy(got, got, sem.at[q, s]).wait()

    def exchange(kind, s):
        start(parts.at[kind], 4 + kind, s, group_peers)
        finish(parts.at[kind], recv, 4 + kind, s, 3)

        @pl.when(tile >= 0)
        def _():
            left = tree_sum([parts[kind, s, r] for r in range(4)]) - images[...]
            for y in range(H):
                line = jnp.broadcast_to(left[y : y + 1, :], (8, W))
                shifts[:, PAD + y * W : PAD + (y + 1) * W] = turn(line, line).astype(BF16)

        finish(parts.at[kind], send, 4 + kind, s, 3)

    def shift_rows(at):
        return jnp.concatenate(
            [shifts[:, at + (10 - a) * W : at + (10 - a) * W + CHUNK] for a in range(TAPS)], axis=0
        )

    def step(s, last):
        exchange(0, s)

        @pl.when(tile >= 0)
        def _():
            total = jnp.zeros((KB, COLS), F32)
            for c in range(PIX // CHUNK):
                at = c * CHUNK
                total = total + nt_dot(held[:, PAD + at : PAD + at + CHUNK], shift_rows(at))
            big = total.astype(BF16)
            rest = total - big.astype(F32)
            mid = rest.astype(BF16)
            small = (rest - mid.astype(F32)).astype(BF16)
            thirds = nt_dot(jnp.concatenate([big, mid, small], axis=0), expand_mat[...])
            total = thirds[0:KB] + (thirds[KB : 2 * KB] + thirds[2 * KB :])
            near[0, s, 0] = total[0:HALF]
            near[1, s, 0] = total[HALF:KB]

        start(near.at[0], 0, s, z_peers)
        start(near.at[1], 1, s, xy_peers)
        finish(near.at[0], recv, 0, s, 7)
        far[0, s, 0] = tree_sum([near[0, s, n] for n in range(8)])
        start(far.at[0], 2, s, xy_peers)
        finish(near.at[1], recv, 1, s, 7)
        far[1, s, 0] = tree_sum([near[1, s, n] for n in range(8)])
        start(far.at[1], 3, s, z_peers)
        for q in range(2):
            finish(near.at[q], send, q, s, 7)
        for q in range(2):
            finish(far.at[q], recv, 2 + q, s, 7)
        gradient = jnp.concatenate(
            [tree_sum([far[q, s, n] for n in range(8)]) for q in range(2)], axis=0
        )
        old = bank[...]
        values = old - step_filter * gradient / 393216.0
        values = values / jnp.sqrt(jnp.sum(values * values, axis=1, keepdims=True) + 1e-06)
        owner = jnp.full((KB, 128), plan[s], jnp.int32) == jnp.full((KB, 128), fblk, jnp.int32)
        bank[...] = jnp.where(owner, values, old)
        for q in range(2):
            finish(far.at[q], send, 2 + q, s, 7)
        synth(1, s)
        exchange(1, s)

        @pl.when(tile >= 0)
        def _():
            weights = jnp.dot(
                bank[...].astype(BF16), expand_mat[...], preferred_element_type=F32
            ).astype(BF16)
            for c in range(PIX // CHUNK):
                at = c * CHUNK
                slope = jnp.dot(weights, shift_rows(at), preferred_element_type=F32)
                value = held[:, PAD + at : PAD + at + CHUNK].astype(F32) - step_code * slope
                value = value - jnp.clip(value, -shrink_level, shrink_level)
                if last:
                    for i in range(ROWS):
                        natural[pl.ds(c * ROWS + i, KB, stride=H), :] = value[:, i * W : (i + 1) * W]
                else:
                    held[:, PAD + at : PAD + at + CHUNK] = value.astype(BF16)

        if not last:
            synth(0, s + 1)

    synth(0, 0)
    pl.semaphore_wait(barrier, len(peers))

    def early_step(s, carry):
        step(s, False)
        return carry

    lax.fori_loop(0, STEPS - 1, early_step, 0)
    step(STEPS - 1, True)
    filters_out[...] = bank[...]

    def fold(k, carry):
        rows = pl.ds(pl.multiple_of(k * 8 * H, 8 * H), 8 * H)
        codes_out[rows, :] = natural[rows, :].astype(BF16)
        return carry

    lax.fori_loop(0, KB // 8, fold, 0)


def body(images, sparse_codes, filters, plan):
    flat_filters = jnp.pad(filters.reshape(KB, 121), ((0, 0), (0, 7)))
    vmem = pl.BlockSpec(memory_space=pltpu.VMEM)
    new_filters, new_codes = pl.pallas_call(
        kernel,
        out_shape=(
            jax.ShapeDtypeStruct((KB, 128), F32),
            jax.ShapeDtypeStruct((KB * H, W), BF16),
        ),
        in_specs=[pl.BlockSpec(memory_space=pltpu.SMEM), vmem, vmem, vmem],
        out_specs=(vmem, vmem),
        scratch_shapes=[
            pltpu.VMEM((KB * H, W), F32),
            pltpu.VMEM((KB, CODE_LANES), BF16),
            pltpu.VMEM((GROUPS * 16, MAP_LANES), F32),
            pltpu.VMEM((4 * GROUPS * 16, 128), BF16),
            pltpu.VMEM((128, COLS), BF16),
            pltpu.VMEM((16, SHIFT_LANES), BF16),
            pltpu.VMEM((KB, 128), F32),
            pltpu.VMEM((2, STEPS, 4, H, W), F32),
            pltpu.VMEM((2, STEPS, 8, HALF, 128), F32),
            pltpu.VMEM((2, STEPS, 8, HALF, 128), F32),
            pltpu.SemaphoreType.DMA((6, STEPS)),
            pltpu.SemaphoreType.DMA((6, STEPS)),
        ],
        compiler_params=pltpu.CompilerParams(
            collective_id=0, has_side_effects=True, vmem_limit_bytes=40 * 1024 * 1024
        ),
        name="coordinate_steps",
    )(plan, images.reshape(H, W), sparse_codes.reshape(KB * H, W), flat_filters)
    return (
        new_filters[:, :121].reshape(KB, TAPS, TAPS),
        new_codes.reshape(1, KB, H, W),
    )


def solution(mesh):
    in_specs = (P("tiles", None, None), P("tiles", "fblk", None, None), P("fblk", None, None), P())
    out_specs = (P("fblk", None, None), P("tiles", "fblk", None, None))
    return jax.shard_map(body, mesh=mesh, in_specs=in_specs, out_specs=out_specs, check_vma=False)
```

time: 1920 us -> 108 us (0.06)
  blocking collectives: 1340 us -> 0 us
  local copies, waits for them, and re-layouts: 508 us -> 4.47 us
  Pallas kernels: 0 us -> 103 us
  other arithmetic: 23 us -> 0 us
  matrix products: 20.1 us -> 0 us
    psum x12 -> x0, blocking collectives: 1340 us -> none  [the longest x4 999 us: body(): grad_sum = lax.psum(grad_part, 'tiles')]
    unnamed x915 -> x7, local copies, waits for them, and re-layouts: 340 us -> 2.74 us
    another operation x76 -> x0, local copies, waits for them, and re-layouts: 141 us -> none  [the longest x68 140 us: shifted(): return jnp.stack(pieces, axis=1).astype(jnp.bfloat16)]
    pallas_call x0 -> x1, Pallas kernels: none -> 103 us  [body(): pl.pallas_call(kernel, out_shape=(jax.ShapeDtypeStruct((KB, 128), F32), j...]
    reshape x11 -> x3, local copies, waits for them, and re-layouts: 26.3 us -> 1.63 us  [the longest x2 0.97 us: body(): flat_filters = jnp.pad(filters.reshape(KB, 121), ((0, 0), (0, 7)))]
    dot_general x16 -> x0, matrix products: 20.1 us -> none  [the longest x8 16 us: synthesize(): jnp.einsum('ko,tkp->top', weights_bf, flat_codes, preferred_element_type=...]
    add x8 -> x0, other arithmetic: 19.3 us -> none  [spread(): summed + padded[:, row_tap * 11 + col_tap, row_tap:row_tap + height, col_...]
where the time goes in v1:
time: 108 us
  Pallas kernels  103 us (95%)
  local copies, waits for them, and re-layouts  4.47 us (4%)
    pallas_call x1, Pallas kernels, body(): pl.pallas_call(kernel, out_shape=(jax.ShapeDtypeStruct((KB, 128), F32), j...  103 us
    unnamed x7, local copies, waits for them, and re-layouts  2.74 us

profile of v1, /device:TPU:1, one launch (start us, length us, event | category | flops | bytes accessed | tf_op | source)
XLA Modules:
  0.0 108.0 jit_solution(11912724152958583615)
XLA Ops:
  0.6 0.9 reshape.21
  1.5 0.1 copy.8
  1.6 0.0 copy-start.1
  1.6 0.0 copy-start.2
  1.6 0.7 copy-done.1
  2.4 0.0 copy-done.2
  2.4 0.0 copy-start
  2.4 1.1 %copy-done = bf16[1,64,48,128]{3,2,1,0:T(8,128)(2,1)S(1)} copy-done((bf16[1,64,48,128]{3,2,1,0:T(8,128)(2,1)S(1)}, bf16[1,64,48,128]{3,2,1,0:T(8,128)(2,1)}, u32[]{:S(2)}) %copy-start) | copy-done | bytes 786456
  3.5 102.8 %coordinate_steps.1 = (f32[64,128]{1,0:T(8,128)S(1)}, bf16[3072,128]{1,0:T(8,128)(2,1)S(1)}) custom-call(s32[4]{0:T(128)S(1)} %copy-done.2, f32[48,128]{1,0:T(8,128)S(1)} %bitcast.11, bf16[3072,128]{1,0:T(8,128)(2,1)S(1)} %bitcast.9, f32[64,128]{1,0:T(8,128)S(1)} %pad.4.filters), custom_call_target="tpu_custom_call" | custom-call | tf_op jit(solution)/shard_map/coordinate_steps/pallas_call | solution.py:251
  106.3 0.1 copy.9
  106.4 0.7 reshape.22
  107.1 0.9 copy.11
  (1 shorter events, 0.0 us)
Async XLA Ops:
  1.6 0.8 copy-start.1
  1.6 0.7 copy-start.2
  2.4 1.1 %copy-start = (bf16[1,64,48,128]{3,2,1,0:T(8,128)(2,1)S(1)}, bf16[1,64,48,128]{3,2,1,0:T(8,128)(2,1)}, u32[]{:S(2)}) copy-start(bf16[1,64,48,128]{3,2,1,0:T(8,128)(2,1)} %param.5) | copy-start | bytes 2359300

commit v2 on v1

--- a/solution.py
+++ b/solution.py
@@ -51,21 +51,35 @@
 
 
 def kernel(
-    plan, images, codes, filters, filters_out, codes_out,
-    natural, held, maps, spread_mat, expand_mat, shifts, bank, parts, near, far, send, recv,
+    plan, images_in, codes_in, filters_in, filters_out, codes_out,
+    images, codes, filters, turned_filters, natural, held, maps, spread_mat, expand_mat, shifts, bank, parts, near, far, send, recv, local,
+    synth_mat, code_mat,
 ):
     tile, fblk = lax.axis_index("tiles"), lax.axis_index("fblk")
     z_peers = [(n, 0) for n in range(1, 8)]
     xy_peers = [(8 * n, 0) for n in range(1, 8)]
     group_peers = [(0, r) for r in range(1, 4)]
     peers = z_peers + xy_peers + group_peers
+    along_z = (z_peers, (4, 3, 5, 6, 2, 7, 1))
+    along_xy = (xy_peers, (5, 4, 7, 3, 6, 2, 1))
+    in_group = (group_peers, (2, 3, 1))
+
+    places = {peer: (flip(tile, peer[0]), flip(fblk, peer[1])) for peer in peers}
 
     def device(peer):
-        return (flip(tile, peer[0]), flip(fblk, peer[1]))
+        return places[peer]
 
     barrier = pltpu.get_barrier_semaphore()
     for peer in peers:
         pl.semaphore_signal(barrier, inc=1, device_id=device(peer), device_id_type=MESH)
+
+    loads = [
+        pltpu.make_async_copy(codes_in, codes, local.at[0]),
+        pltpu.make_async_copy(filters_in, filters, local.at[1]),
+        pltpu.make_async_copy(images_in, images, local.at[2]),
+    ]
+    for load in loads:
+        load.start()
 
     row = lax.broadcasted_iota(jnp.int32, (4 * GROUPS * 16, 128), 0)
     col = lax.broadcasted_iota(jnp.int32, (4 * GROUPS * 16, 128), 1)
@@ -86,7 +100,12 @@
     held[:, PAD + PIX : CODE_LANES] = jnp.zeros((KB, CODE_LANES - PAD - PIX), BF16)
     shifts[:, 0:PAD] = jnp.zeros((16, PAD), BF16)
     shifts[:, PAD + PIX : SHIFT_LANES] = jnp.zeros((16, PAD), BF16)
-    bank[...] = filters[...]
+    for load in loads:
+        load.wait()
+    turned_filters[...] = jnp.zeros((128, 128), F32)
+    for a in range(TAPS):
+        turned_filters[a * TAPS : (a + 1) * TAPS, 0:KB] = filters[a]
+    bank[...] = jnp.transpose(turned_filters[...])[0:KB, :]
 
     def unfold(k, carry):
         rows = pl.ds(pl.multiple_of(k * 8 * H, 8 * H), 8 * H)
@@ -107,13 +126,16 @@
         back = pltpu.roll(back, W - 8, 1, stride=1, stride_axis=0)
         return jnp.where(inside, jnp.concatenate([front, back], axis=0), 0.0)
 
+    def set_synth_mat():
+        slabs = nt_dot(spread_mat[...], bank[...].astype(BF16))
+        synth_mat[...] = jnp.concatenate(
+            [slabs[r * GROUPS * 16 : (r + 1) * GROUPS * 16] for r in range(4)], axis=1
+        ).astype(BF16)
+
     def synth(kind, s):
         @pl.when(tile >= 0)
         def _():
-            slabs = nt_dot(spread_mat[...], bank[...].astype(BF16))
-            weights = jnp.concatenate(
-                [slabs[r * GROUPS * 16 : (r + 1) * GROUPS * 16] for r in range(4)], axis=1
-            ).astype(BF16)
+            weights = synth_mat[...]
             lag = 3
             for c in range(H // ROWS + lag):
                 at = c * CHUNK
@@ -139,15 +161,16 @@
         )
 
     def start(ref, q, s, targets):
-        for n, peer in enumerate(targets):
-            copies(ref, ref, q, s, n + 1, peer).start()
+        for n in targets[1]:
+            copies(ref, ref, q, s, n, targets[0][n - 1]).start()
 
     def finish(ref, sem, q, s, count):
         got = ref.at[s, pl.ds(1, count)]
         pltpu.make_async_copy(got, got, sem.at[q, s]).wait()
 
-    def exchange(kind, s):
-        start(parts.at[kind], 4 + kind, s, group_peers)
+    def exchange(kind, s, meanwhile):
+        start(parts.at[kind], 4 + kind, s, in_group)
+        pl.when(tile >= 0)(meanwhile)
         finish(parts.at[kind], recv, 4 + kind, s, 3)
 
         @pl.when(tile >= 0)
@@ -157,15 +180,19 @@
                 line = jnp.broadcast_to(left[y : y + 1, :], (8, W))
                 shifts[:, PAD + y * W : PAD + (y + 1) * W] = turn(line, line).astype(BF16)
 
-        finish(parts.at[kind], send, 4 + kind, s, 3)
 
     def shift_rows(at):
         return jnp.concatenate(
             [shifts[:, at + (10 - a) * W : at + (10 - a) * W + CHUNK] for a in range(TAPS)], axis=0
         )
 
+    def set_code_mat():
+        code_mat[...] = jnp.dot(
+            bank[...].astype(BF16), expand_mat[...], preferred_element_type=F32
+        ).astype(BF16)
+
     def step(s, last):
-        exchange(0, s)
+        exchange(0, s, lambda: None)
 
         @pl.when(tile >= 0)
         def _():
@@ -182,16 +209,14 @@
             near[0, s, 0] = total[0:HALF]
             near[1, s, 0] = total[HALF:KB]
 
-        start(near.at[0], 0, s, z_peers)
-        start(near.at[1], 1, s, xy_peers)
+        start(near.at[0], 0, s, along_z)
+        start(near.at[1], 1, s, along_xy)
+        finish(near.at[1], recv, 1, s, 7)
+        far[1, s, 0] = tree_sum([near[1, s, n] for n in range(8)])
+        start(far.at[1], 3, s, along_z)
         finish(near.at[0], recv, 0, s, 7)
         far[0, s, 0] = tree_sum([near[0, s, n] for n in range(8)])
-        start(far.at[0], 2, s, xy_peers)
-        finish(near.at[1], recv, 1, s, 7)
-        far[1, s, 0] = tree_sum([near[1, s, n] for n in range(8)])
-        start(far.at[1], 3, s, z_peers)
-        for q in range(2):
-            finish(near.at[q], send, q, s, 7)
+        start(far.at[0], 2, s, along_xy)
         for q in range(2):
             finish(far.at[q], recv, 2 + q, s, 7)
         gradient = jnp.concatenate(
@@ -202,16 +227,13 @@
         values = values / jnp.sqrt(jnp.sum(values * values, axis=1, keepdims=True) + 1e-06)
         owner = jnp.full((KB, 128), plan[s], jnp.int32) == jnp.full((KB, 128), fblk, jnp.int32)
         bank[...] = jnp.where(owner, values, old)
-        for q in range(2):
-            finish(far.at[q], send, 2 + q, s, 7)
+        set_synth_mat()
         synth(1, s)
-        exchange(1, s)
+        exchange(1, s, set_code_mat)
 
         @pl.when(tile >= 0)
         def _():
-            weights = jnp.dot(
-                bank[...].astype(BF16), expand_mat[...], preferred_element_type=F32
-            ).astype(BF16)
+            weights = code_mat[...]
             for c in range(PIX // CHUNK):
                 at = c * CHUNK
                 slope = jnp.dot(weights, shift_rows(at), preferred_element_type=F32)
@@ -226,6 +248,7 @@
         if not last:
             synth(0, s + 1)
 
+    set_synth_mat()
     synth(0, 0)
     pl.semaphore_wait(barrier, len(peers))
 
@@ -235,7 +258,15 @@
 
     lax.fori_loop(0, STEPS - 1, early_step, 0)
     step(STEPS - 1, True)
-    filters_out[...] = bank[...]
+    for s in range(STEPS):
+        for q in range(2):
+            finish(near.at[q], send, q, s, 7)
+            finish(far.at[q], send, 2 + q, s, 7)
+            finish(parts.at[q], send, 4 + q, s, 3)
+    turned_filters[0:KB, :] = bank[...]
+    turned_filters[...] = jnp.transpose(turned_filters[...])
+    for a in range(TAPS):
+        filters_out[a] = turned_filters[a * TAPS : (a + 1) * TAPS, 0:KB]
 
     def fold(k, carry):
         rows = pl.ds(pl.multiple_of(k * 8 * H, 8 * H), 8 * H)
@@ -246,17 +277,21 @@
 
 
 def body(images, sparse_codes, filters, plan):
-    flat_filters = jnp.pad(filters.reshape(KB, 121), ((0, 0), (0, 7)))
     vmem = pl.BlockSpec(memory_space=pltpu.VMEM)
+    hbm = pl.BlockSpec(memory_space=pltpu.HBM)
     new_filters, new_codes = pl.pallas_call(
         kernel,
         out_shape=(
-            jax.ShapeDtypeStruct((KB, 128), F32),
+            jax.ShapeDtypeStruct((TAPS, TAPS, KB), F32),
             jax.ShapeDtypeStruct((KB * H, W), BF16),
         ),
-        in_specs=[pl.BlockSpec(memory_space=pltpu.SMEM), vmem, vmem, vmem],
+        in_specs=[pl.BlockSpec(memory_space=pltpu.SMEM), hbm, hbm, hbm],
         out_specs=(vmem, vmem),
         scratch_shapes=[
+            pltpu.VMEM((H, W), F32),
+            pltpu.VMEM((KB * H, W), BF16),
+            pltpu.VMEM((TAPS, TAPS, KB), F32),
+            pltpu.VMEM((128, 128), F32),
             pltpu.VMEM((KB * H, W), F32),
             pltpu.VMEM((KB, CODE_LANES), BF16),
             pltpu.VMEM((GROUPS * 16, MAP_LANES), F32),
@@ -269,14 +304,17 @@
             pltpu.VMEM((2, STEPS, 8, HALF, 128), F32),
             pltpu.SemaphoreType.DMA((6, STEPS)),
             pltpu.SemaphoreType.DMA((6, STEPS)),
+            pltpu.SemaphoreType.DMA((3,)),
+            pltpu.VMEM((GROUPS * 16, 4 * KB), BF16),
+            pltpu.VMEM((KB, COLS), BF16),
         ],
         compiler_params=pltpu.CompilerParams(
-            collective_id=0, has_side_effects=True, vmem_limit_bytes=40 * 1024 * 1024
+            collective_id=0, has_side_effects=True, vmem_limit_bytes=52 * 1024 * 1024 + 512 * 1024
         ),
         name="coordinate_steps",
-    )(plan, images.reshape(H, W), sparse_codes.reshape(KB * H, W), flat_filters)
+    )(plan, images.reshape(H, W), sparse_codes.reshape(KB * H, W), filters.transpose(1, 2, 0))
     return (
-        new_filters[:, :121].reshape(KB, TAPS, TAPS),
+        new_filters.transpose(2, 0, 1),
         new_codes.reshape(1, KB, H, W),
     )
 

time: 108 us -> 98 us (0.907)
  Pallas kernels: 103 us -> 93.3 us
    pallas_call x1, Pallas kernels: 103 us -> 93.3 us  [body(): pl.pallas_call(kernel, out_shape=(jax.ShapeDtypeStruct((TAPS, TAPS, KB),...]
    reshape x3 -> x0, local copies, waits for them, and re-layouts: 1.63 us -> none  [the longest x2 0.97 us: body(): flat_filters = jnp.pad(filters.reshape(KB, 121), ((0, 0), (0, 7)))]
    unnamed x7 -> x8, local copies, waits for them, and re-layouts: 2.74 us -> 3.79 us
where the time goes in v2:
time: 98 us; the launch traced here: 97.8 us
  Pallas kernels  93.3 us (95%)
  local copies, waits for them, and re-layouts  3.79 us (4%)
    pallas_call x1, Pallas kernels, body(): pl.pallas_call(kernel, out_shape=(jax.ShapeDtypeStruct((TAPS, TAPS, KB),...  93.3 us
    unnamed x8, local copies, waits for them, and re-layouts  3.79 us

profile of v2, /device:TPU:1, one launch (start us, length us, event | category | flops | bytes accessed | tf_op | source)
XLA Modules:
  0.0 97.8 jit_solution(3705422906154088786)
XLA Ops:
  0.6 0.0 copy-start.2
  0.6 0.6 copy-done.2
  1.3 0.0 copy-start
  1.3 0.9 copy-done
  2.2 0.0 copy-start.1
  2.2 0.7 copy-done.1
  2.9 93.3 %coordinate_steps.1 = (f32[11,11,64]{2,1,0:T(8,128)S(1)}, bf16[3072,128]{1,0:T(8,128)(2,1)S(1)}) custom-call(s32[4]{0:T(128)S(1)} %copy-done.2, f32[48,128]{1,0:T(8,128)S(1)} %bitcast.8, bf16[3072,128]{1,0:T(8,128)(2,1)} %bitcast.9, f32[11,11,64]{2,1,0:T(8,128)S(1)} %bitcast.6), custom_call_target="tpu_custom_call" | custom-call | tf_op jit(solution)/shard_map/coordinate_steps/pallas_call | solution.py:282
  96.2 0.6 copy.8
  96.9 0.9 copy.9
Async XLA Ops:
  0.6 0.7 copy-start.2
  1.3 0.9 copy-start
  2.2 0.7 copy-start.1

commit v3 on v2

--- a/solution.py
+++ b/solution.py
@@ -19,6 +19,8 @@
 MAP_LANES = 56 * W
 CHUNK = 512
 ROWS = CHUNK // W
+UPPER = H // 2
+EARLY = (UPPER - 5) // ROWS
 
 step_filter = 128.0
 step_code = 0.05
@@ -53,7 +55,7 @@
 def kernel(
     plan, images_in, codes_in, filters_in, filters_out, codes_out,
     images, codes, filters, turned_filters, natural, held, maps, spread_mat, expand_mat, shifts, bank, parts, near, far, send, recv, local,
-    synth_mat, code_mat,
+    synth_mat, code_mat, early_grad,
 ):
     tile, fblk = lax.axis_index("tiles"), lax.axis_index("fblk")
     z_peers = [(n, 0) for n in range(1, 8)]
@@ -64,13 +66,17 @@
     along_xy = (xy_peers, (5, 4, 7, 3, 6, 2, 1))
     in_group = (group_peers, (2, 3, 1))
 
+    farthest_first = [
+        group[n - 1] for group, n in [(z_peers, n) for n in along_z[1]] + [(xy_peers, n) for n in along_xy[1]]
+        + [(group_peers, n) for n in in_group[1]]
+    ]
     places = {peer: (flip(tile, peer[0]), flip(fblk, peer[1])) for peer in peers}
 
     def device(peer):
         return places[peer]
 
     barrier = pltpu.get_barrier_semaphore()
-    for peer in peers:
+    for peer in farthest_first:
         pl.semaphore_signal(barrier, inc=1, device_id=device(peer), device_id_type=MESH)
 
     loads = [
@@ -132,12 +138,13 @@
             [slabs[r * GROUPS * 16 : (r + 1) * GROUPS * 16] for r in range(4)], axis=1
         ).astype(BF16)
 
-    def synth(kind, s):
+    def synth(kind, s, half):
         @pl.when(tile >= 0)
         def _():
             weights = synth_mat[...]
             lag = 3
-            for c in range(H // ROWS + lag):
+            middle, end = UPPER // ROWS + lag, H // ROWS + lag
+            for c in range(middle) if half == 0 else range(middle, end):
                 at = c * CHUNK
                 if at < MAP_LANES:
                     piled = jnp.concatenate(
@@ -168,18 +175,38 @@
         got = ref.at[s, pl.ds(1, count)]
         pltpu.make_async_copy(got, got, sem.at[q, s]).wait()
 
-    def exchange(kind, s, meanwhile):
-        start(parts.at[kind], 4 + kind, s, in_group)
-        pl.when(tile >= 0)(meanwhile)
-        finish(parts.at[kind], recv, 4 + kind, s, 3)
-
-        @pl.when(tile >= 0)
-        def _():
-            left = tree_sum([parts[kind, s, r] for r in range(4)]) - images[...]
-            for y in range(H):
-                line = jnp.broadcast_to(left[y : y + 1, :], (8, W))
-                shifts[:, PAD + y * W : PAD + (y + 1) * W] = turn(line, line).astype(BF16)
-
+    def send_parts(kind, s, half):
+        rows = pl.ds(half * UPPER, UPPER)
+        for n in in_group[1]:
+            pltpu.make_async_remote_copy(
+                src_ref=parts.at[kind, s, 0, rows], dst_ref=parts.at[kind, s, n, rows],
+                send_sem=send.at[4 + 2 * kind + half, s], recv_sem=recv.at[4 + 2 * kind + half, s],
+                device_id=device(group_peers[n - 1]), device_id_type=MESH,
+            ).start()
+
+    def finish_parts(sem, kind, s, half):
+        got = parts.at[kind, s, pl.ds(1, 3), pl.ds(half * UPPER, UPPER)]
+        pltpu.make_async_copy(got, got, sem.at[4 + 2 * kind + half, s]).wait()
+
+    def synth_and_send(kind, s):
+        for half in range(2):
+            synth(kind, s, half)
+            send_parts(kind, s, half)
+
+    def exchange(kind, s, work):
+        for half in range(2):
+            finish_parts(recv, kind, s, half)
+
+            @pl.when(tile >= 0)
+            def _():
+                first = half * UPPER
+                rows = slice(first, first + UPPER)
+                left = tree_sum([parts[kind, s, r, rows] for r in range(4)]) - images[rows, :]
+                for y in range(UPPER):
+                    line = jnp.broadcast_to(left[y : y + 1, :], (8, W))
+                    at = PAD + (first + y) * W
+                    shifts[:, at : at + W] = turn(line, line).astype(BF16)
+                work(half, range(EARLY) if half == 0 else range(EARLY, PIX // CHUNK))
 
     def shift_rows(at):
         return jnp.concatenate(
@@ -192,25 +219,28 @@
         ).astype(BF16)
 
     def step(s, last):
-        exchange(0, s, lambda: None)
-
-        @pl.when(tile >= 0)
-        def _():
-            total = jnp.zeros((KB, COLS), F32)
-            for c in range(PIX // CHUNK):
+        def to_gradient(half, chunks):
+            total = jnp.zeros((KB, COLS), F32) if half == 0 else early_grad[...]
+            for c in chunks:
                 at = c * CHUNK
                 total = total + nt_dot(held[:, PAD + at : PAD + at + CHUNK], shift_rows(at))
+            if half == 0:
+                early_grad[...] = total
+                return
             big = total.astype(BF16)
             rest = total - big.astype(F32)
             mid = rest.astype(BF16)
             small = (rest - mid.astype(F32)).astype(BF16)
-            thirds = nt_dot(jnp.concatenate([big, mid, small], axis=0), expand_mat[...])
-            total = thirds[0:KB] + (thirds[KB : 2 * KB] + thirds[2 * KB :])
-            near[0, s, 0] = total[0:HALF]
-            near[1, s, 0] = total[HALF:KB]
-
-        start(near.at[0], 0, s, along_z)
-        start(near.at[1], 1, s, along_xy)
+            for q in range(2):
+                part = slice(q * HALF, (q + 1) * HALF)
+                thirds = nt_dot(
+                    jnp.concatenate([big[part], mid[part], small[part]], axis=0), expand_mat[...]
+                )
+                near[q, s, 0] = thirds[0:HALF] + (thirds[HALF : 2 * HALF] + thirds[2 * HALF :])
+                start(near.at[q], q, s, (along_z, along_xy)[q])
+
+        exchange(0, s, to_gradient)
+
         finish(near.at[1], recv, 1, s, 7)
         far[1, s, 0] = tree_sum([near[1, s, n] for n in range(8)])
         start(far.at[1], 3, s, along_z)
@@ -228,13 +258,12 @@
         owner = jnp.full((KB, 128), plan[s], jnp.int32) == jnp.full((KB, 128), fblk, jnp.int32)
         bank[...] = jnp.where(owner, values, old)
         set_synth_mat()
-        synth(1, s)
-        exchange(1, s, set_code_mat)
-
-        @pl.when(tile >= 0)
-        def _():
+        synth_and_send(1, s)
+        pl.when(tile >= 0)(set_code_mat)
+
+        def to_codes(half, chunks):
             weights = code_mat[...]
-            for c in range(PIX // CHUNK):
+            for c in chunks:
                 at = c * CHUNK
                 slope = jnp.dot(weights, shift_rows(at), preferred_element_type=F32)
                 value = held[:, PAD + at : PAD + at + CHUNK].astype(F32) - step_code * slope
@@ -245,12 +274,16 @@
                 else:
                     held[:, PAD + at : PAD + at + CHUNK] = value.astype(BF16)
 
+        exchange(1, s, to_codes)
         if not last:
-            synth(0, s + 1)
+            synth_and_send(0, s + 1)
 
     set_synth_mat()
-    synth(0, 0)
+    for half in range(2):
+        synth(0, 0, half)
     pl.semaphore_wait(barrier, len(peers))
+    for half in range(2):
+        send_parts(0, 0, half)
 
     def early_step(s, carry):
         step(s, False)
@@ -262,7 +295,8 @@
         for q in range(2):
             finish(near.at[q], send, q, s, 7)
             finish(far.at[q], send, 2 + q, s, 7)
-            finish(parts.at[q], send, 4 + q, s, 3)
+            for half in range(2):
+                finish_parts(send, q, s, half)
     turned_filters[0:KB, :] = bank[...]
     turned_filters[...] = jnp.transpose(turned_filters[...])
     for a in range(TAPS):
@@ -302,11 +336,12 @@
             pltpu.VMEM((2, STEPS, 4, H, W), F32),
             pltpu.VMEM((2, STEPS, 8, HALF, 128), F32),
             pltpu.VMEM((2, STEPS, 8, HALF, 128), F32),
-            pltpu.SemaphoreType.DMA((6, STEPS)),
-            pltpu.SemaphoreType.DMA((6, STEPS)),
+            pltpu.SemaphoreType.DMA((8, STEPS)),
+            pltpu.SemaphoreType.DMA((8, STEPS)),
             pltpu.SemaphoreType.DMA((3,)),
             pltpu.VMEM((GROUPS * 16, 4 * KB), BF16),
             pltpu.VMEM((KB, COLS), BF16),
+            pltpu.VMEM((KB, COLS), F32),
         ],
         compiler_params=pltpu.CompilerParams(
             collective_id=0, has_side_effects=True, vmem_limit_bytes=52 * 1024 * 1024 + 512 * 1024

time: 98 us -> 97.8 us (level)
  no operation moved by 1% of the time
where the time goes in v3:
time: 97.8 us; the launch traced here: 97.5 us
  Pallas kernels  93.1 us (95%)
  local copies, waits for them, and re-layouts  3.79 us (4%)
    pallas_call x1, Pallas kernels, body(): pl.pallas_call(kernel, out_shape=(jax.ShapeDtypeStruct((TAPS, TAPS, KB),...  93.1 us
    unnamed x8, local copies, waits for them, and re-layouts  3.79 us

profile of v3, /device:TPU:1, one launch (start us, length us, event | category | flops | bytes accessed | tf_op | source)
XLA Modules:
  0.0 97.5 jit_solution(9246391971077709001)
XLA Ops:
  0.6 0.0 copy-start.2
  0.6 0.6 copy-done.2
  1.3 0.0 copy-start
  1.3 0.9 copy-done
  2.2 0.0 copy-start.1
  2.2 0.7 copy-done.1
  2.9 93.1 %coordinate_steps.1 = (f32[11,11,64]{2,1,0:T(8,128)S(1)}, bf16[3072,128]{1,0:T(8,128)(2,1)S(1)}) custom-call(s32[4]{0:T(128)S(1)} %copy-done.2, f32[48,128]{1,0:T(8,128)S(1)} %bitcast.8, bf16[3072,128]{1,0:T(8,128)(2,1)} %bitcast.9, f32[11,11,64]{2,1,0:T(8,128)S(1)} %bitcast.6), custom_call_target="tpu_custom_call" | custom-call | tf_op jit(solution)/shard_map/coordinate_steps/pallas_call | solution.py:316
  96.0 0.6 copy.8
  96.7 0.9 copy.9
Async XLA Ops:
  0.6 0.7 copy-start.2
  1.3 0.9 copy-start
  2.2 0.7 copy-start.1

commit v4 on v3

--- a/solution.py
+++ b/solution.py
@@ -218,7 +218,7 @@
             bank[...].astype(BF16), expand_mat[...], preferred_element_type=F32
         ).astype(BF16)
 
-    def step(s, last):
+    def step(s, carry):
         def to_gradient(half, chunks):
             total = jnp.zeros((KB, COLS), F32) if half == 0 else early_grad[...]
             for c in chunks:
@@ -239,6 +239,7 @@
                 near[q, s, 0] = thirds[0:HALF] + (thirds[HALF : 2 * HALF] + thirds[2 * HALF :])
                 start(near.at[q], q, s, (along_z, along_xy)[q])
 
+        synth_and_send(0, s)
         exchange(0, s, to_gradient)
 
         finish(near.at[1], recv, 1, s, 7)
@@ -268,29 +269,17 @@
                 slope = jnp.dot(weights, shift_rows(at), preferred_element_type=F32)
                 value = held[:, PAD + at : PAD + at + CHUNK].astype(F32) - step_code * slope
                 value = value - jnp.clip(value, -shrink_level, shrink_level)
-                if last:
-                    for i in range(ROWS):
-                        natural[pl.ds(c * ROWS + i, KB, stride=H), :] = value[:, i * W : (i + 1) * W]
-                else:
-                    held[:, PAD + at : PAD + at + CHUNK] = value.astype(BF16)
+                held[:, PAD + at : PAD + at + CHUNK] = value.astype(BF16)
 
         exchange(1, s, to_codes)
-        if not last:
-            synth_and_send(0, s + 1)
+        return carry
 
     set_synth_mat()
-    for half in range(2):
-        synth(0, 0, half)
     pl.semaphore_wait(barrier, len(peers))
-    for half in range(2):
-        send_parts(0, 0, half)
-
-    def early_step(s, carry):
-        step(s, False)
-        return carry
-
-    lax.fori_loop(0, STEPS - 1, early_step, 0)
-    step(STEPS - 1, True)
+
+    lax.fori_loop(0, STEPS, step, 0)
+    for y in range(H):
+        natural[pl.ds(y, KB, stride=H), :] = held[:, PAD + y * W : PAD + (y + 1) * W].astype(F32)
     for s in range(STEPS):
         for q in range(2):
             finish(near.at[q], send, q, s, 7)

time: 97.8 us -> 98.9 us (1.011)
  Pallas kernels: 93.1 us -> 94.2 us
    pallas_call x1, Pallas kernels: 93.1 us -> 94.2 us  [body(): pl.pallas_call(kernel, out_shape=(jax.ShapeDtypeStruct((TAPS, TAPS, KB),...]
where the time goes in v4:
time: 98.9 us; the launch traced here: 98.6 us
  Pallas kernels  94.2 us (95%)
  local copies, waits for them, and re-layouts  3.79 us (4%)
    pallas_call x1, Pallas kernels, body(): pl.pallas_call(kernel, out_shape=(jax.ShapeDtypeStruct((TAPS, TAPS, KB),...  94.2 us
    unnamed x8, local copies, waits for them, and re-layouts  3.79 us

profile of v4, /device:TPU:1, one launch (start us, length us, event | category | flops | bytes accessed | tf_op | source)
XLA Modules:
  0.0 98.6 jit_solution(10610179859079247751)
XLA Ops:
  0.6 0.0 copy-start.2
  0.6 0.6 copy-done.2
  1.3 0.0 copy-start
  1.3 0.9 copy-done
  2.2 0.0 copy-start.1
  2.2 0.7 copy-done.1
  2.9 94.2 %coordinate_steps.1 = (f32[11,11,64]{2,1,0:T(8,128)S(1)}, bf16[3072,128]{1,0:T(8,128)(2,1)S(1)}) custom-call(s32[4]{0:T(128)S(1)} %copy-done.2, f32[48,128]{1,0:T(8,128)S(1)} %bitcast.8, bf16[3072,128]{1,0:T(8,128)(2,1)} %bitcast.9, f32[11,11,64]{2,1,0:T(8,128)S(1)} %bitcast.6), custom_call_target="tpu_custom_call" | custom-call | tf_op jit(solution)/shard_map/coordinate_steps/pallas_call | solution.py:305
  97.1 0.6 copy.8
  97.8 0.9 copy.9
Async XLA Ops:
  0.6 0.7 copy-start.2
  1.3 0.9 copy-start
  2.2 0.7 copy-start.1
